TPU v7x, 32 devices: a whole 2x2x4 slice. The times are simulated.
32 devices in a mesh: gx: 4 (over z), gy: 4 (over y, x), gz: 2 (over core).
Axes of the slice: x: 2, y: 2, z: 4, core: 2. Of those that a mesh axis runs over, the one named last changes fastest.
Arguments:
- species_partial_mass: float32 [9, 16, 128, 512], P(None, 'gz', 'gx', 'gy'), may hold values from 0.2 to 2
- motion_components: float32 [2, 16, 128, 512], P(None, 'gz', 'gx', 'gy'), may hold values from -6 to 6
- grid_stretch_main: float32 [2, 16, 128, 512], P(None, 'gz', 'gx', 'gy'), may hold values from 0.5 to 1.5
- grid_stretch_cross: float32 [2, 16, 128, 512], P(None, 'gz', 'gx', 'gy'), may hold values from -1.2 to 1.2
- volume_scaling_reciprocal: float32 [16, 128, 512], P('gz', 'gx', 'gy'), may hold values from 0.5 to 2
- kelvin_field: float32 [16, 128, 512], P('gz', 'gx', 'gy'), may hold values from 900 to 2500
- first_dir_piece_solver: float32 [32, 32], replicated, may hold values from -1 to 1
- first_dir_rhs_condense: float32 [4, 32], replicated, may hold values from -1 to 1
- first_dir_border_spread: float32 [32, 4], replicated, may hold values from -3 to 3
- first_dir_small_solver: float32 [16, 16], P('gx'), may hold values from -1 to 2
- second_dir_piece_solver: float32 [128, 128], replicated, may hold values from -0.5 to 0.5
- second_dir_rhs_condense: float32 [4, 128], replicated, may hold values from -0.5 to 0.5
- second_dir_border_spread: float32 [128, 4], replicated, may hold values from -3 to 3
- second_dir_small_solver: float32 [16, 16], P('gy'), may hold values from -2 to 3
- speed_factor_ln_reference: float32 [19], replicated, may hold values from -1 to 1
- kelvin_exponent_each: float32 [19], replicated, may hold values from -1 to 1
- arrhenius_energy_kelvin: float32 [19], replicated, may hold values from 0 to 6000
- consumed_species_flags: int32 [19, 9], replicated, may hold values 0 or 1
- stoich_net_shift: int32 [19, 9], replicated, may hold values from -2 to 2
- boundary_supplying_volume: int32 [4, 4, 512], P('gx', 'gy', 'gz'), may hold values from 0 to 32767
- boundary_target_volume: int32 [4, 4, 512], P('gx', 'gy', 'gz'), may hold values from 0 to 32767
- boundary_slot_used: int32 [4, 4, 512], P('gx', 'gy', 'gz'), may hold values 0 or 1
- boundary_transfer_weight: float32 [4, 4, 512], P('gx', 'gy', 'gz'), may hold values from 0.2 to 2
- open_volume_flags: int32 [16, 128, 512], P('gz', 'gx', 'gy'), may hold values 0 or 1
Outputs:
- section_rhs: float32 [9, 16, 128, 512], P(None, 'gz', 'gx', 'gy')
- section_state: float32 [9, 16, 128, 512], P(None, 'gz', 'gx', 'gy')
All inputs are finite; a program needn't handle non-finite values. No bound on the sum of `boundary_slot_used` or of `open_volume_flags` on one device may be relied on, other than what follows from the above.
Results may differ from a plain program's by a relative error of at most 0.000068.
Values sent between devices are 32-bit elements; how exact they have to be, the bound alone decides.
A program may use at most 128 MiB of HBM per device.

v0:
```python
import jax
import jax.numpy as jnp
from jax import lax
from jax.sharding import PartitionSpec as P

HI = lax.Precision.HIGHEST


def swapped(value, axis, stride):
    mask = 2**stride
    pairs = [(source, source ^ mask) for source in range(lax.axis_size(axis))]
    return lax.ppermute(value, axis, pairs)


def wall_exchange(outgoing):
    return swapped(outgoing, "gz", 0)


def per_device(
    species_partial_mass,
    motion_components,
    grid_stretch_main,
    grid_stretch_cross,
    volume_scaling_reciprocal,
    kelvin_field,
    first_dir_piece_solver,
    first_dir_rhs_condense,
    first_dir_border_spread,
    first_dir_small_solver,
    second_dir_piece_solver,
    second_dir_rhs_condense,
    second_dir_border_spread,
    second_dir_small_solver,
    speed_factor_ln_reference,
    kelvin_exponent_each,
    arrhenius_energy_kelvin,
    consumed_species_flags,
    stoich_net_shift,
    boundary_supplying_volume,
    boundary_target_volume,
    boundary_slot_used,
    boundary_transfer_weight,
    open_volume_flags,
):
    species, planes, rows_x, rows_y = species_partial_mass.shape
    flat = species_partial_mass.reshape(species, planes * rows_x * rows_y)
    source_cells = boundary_supplying_volume.reshape(-1)
    target_cells = boundary_target_volume.reshape(-1)
    weight = boundary_transfer_weight.reshape(-1) * boundary_slot_used.reshape(-1).astype(
        jnp.float32
    )
    outgoing = flat[:, source_cells] * weight[None, :]
    contra_x = (
        grid_stretch_main[0] * motion_components[0] + grid_stretch_cross[0] * motion_components[1]
    )
    contra_y = (
        grid_stretch_cross[1] * motion_components[0] + grid_stretch_main[1] * motion_components[1]
    )
    flux_x = contra_x[None] * species_partial_mass
    flux_y = contra_y[None] * species_partial_mass
    local_x = jnp.einsum("ab,nzby->nzay", first_dir_piece_solver, flux_x, precision=HI)
    side_x = jnp.einsum("kb,nzby->knzy", first_dir_rhs_condense, flux_x, precision=HI)
    whole_x = lax.all_gather(side_x, "gx", axis=0, tiled=True)
    solved_x = jnp.einsum("ij,jnzy->inzy", first_dir_small_solver, whole_x, precision=HI)
    deriv_x = local_x + jnp.einsum("ak,knzy->nzay", first_dir_border_spread, solved_x, precision=HI)
    local_y = jnp.einsum("ab,nzxb->nzxa", second_dir_piece_solver, flux_y, precision=HI)
    side_y = jnp.einsum("kb,nzxb->nzxk", second_dir_rhs_condense, flux_y, precision=HI)
    whole_y = lax.all_gather(side_y, "gy", axis=3, tiled=True)
    solved_y = jnp.einsum("ij,nzxj->nzxi", second_dir_small_solver, whole_y, precision=HI)
    deriv_y = local_y + jnp.einsum(
        "ak,nzxk->nzxa", second_dir_border_spread, solved_y, precision=HI
    )
    kelvin_natural_ln = jnp.log(kelvin_field / 1500.0)
    reciprocal_kelvin = 1.0 / kelvin_field - 1.0 / 1500.0
    natural_speed_exponent = (
        speed_factor_ln_reference[:, None, None, None]
        + kelvin_exponent_each[:, None, None, None] * kelvin_natural_ln[None]
        - arrhenius_energy_kelvin[:, None, None, None] * reciprocal_kelvin[None]
    )
    log_conc = jnp.log(species_partial_mass)
    progress = jnp.exp(
        natural_speed_exponent
        + jnp.einsum(
            "rn,nzxy->rzxy", consumed_species_flags.astype(jnp.float32), log_conc, precision=HI
        )
    )
    source = 0.2 * jnp.einsum(
        "rn,rzxy->nzxy", stoich_net_shift.astype(jnp.float32), progress, precision=HI
    )
    incoming = wall_exchange(outgoing)
    wall = jnp.zeros_like(flat)
    wall = wall.at[:, target_cells].add(incoming)
    wall = wall.at[:, source_cells].add(-outgoing)
    wall = wall.reshape(species_partial_mass.shape)
    section_rhs = open_volume_flags.astype(jnp.float32)[None] * (
        source + wall - volume_scaling_reciprocal[None] * (deriv_x + deriv_y)
    )
    section_state = species_partial_mass + 0.25 * section_rhs
    return (section_rhs, section_state)


def solution(mesh):
    in_specs = (
        P(None, "gz", "gx", "gy"),
        P(None, "gz", "gx", "gy"),
        P(None, "gz", "gx", "gy"),
        P(None, "gz", "gx", "gy"),
        P("gz", "gx", "gy"),
        P("gz", "gx", "gy"),
        P(),
        P(),
        P(),
        P("gx", None),
        P(),
        P(),
        P(),
        P("gy", None),
        P(),
        P(),
        P(),
        P(),
        P(),
        P("gx", "gy", "gz"),
        P("gx", "gy", "gz"),
        P("gx", "gy", "gz"),
        P("gx", "gy", "gz"),
        P("gz", "gx", "gy"),
    )
    out_specs = (P(None, "gz", "gx", "gy"), P(None, "gz", "gx", "gy"))
    return jax.shard_map(
        per_device, mesh=mesh, in_specs=in_specs, out_specs=out_specs, check_vma=False
    )
```

profile of v0, /device:TPU:0, one launch (start us, length us, event | category | flops | bytes accessed | tf_op | source)
XLA Modules:
  0.0 106.5 jit_solution(7917420916370213954)
XLA Ops:
  0.6 0.0 copy-start
  0.6 0.7 compare_select_fusion
  1.4 0.0 copy-start.18
  1.4 0.0 copy-start.1
  1.4 10.1 %copy.61 = f32[9,8,32,128]{0,3,2,1:T(8,128)} copy(f32[9,8,32,128]{3,2,1,0:T(8,128)} %param.24) | data formatting | bytes 2359296 | tf_op args[0]
  11.5 6.5 %gather_fusion = f32[256,9]{1,0:T(8,128)S(1)} fusion(f32[9,32768]{0,1:T(8,128)} %bitcast.89, s32[1024]{0:T(1024)S(1)} %pad_clamp_fusion), kind=kCustom, calls=%fused_computation | custom fusion | bytes 19456 | tf_op jit(solution)/shard_map/gather | solution.py:52
  18.0 0.1 multiply_bitcast_fusion
  18.1 0.0 copy-start.3
  18.1 0.0 copy-start.4
  18.1 0.0 copy-start.5
  18.2 0.0 copy-start.8
  18.2 0.5 collective-permute-start
  18.7 0.2 log.7
  18.9 0.2 copy-done.3
  19.1 0.1 copy-done.4
  19.2 0.1 copy-done.5
  19.2 0.1 add_bitcast_fusion
  19.3 0.0 copy-start.11
  19.3 1.2 %fusion.26 = f32[9,8,128,32]{2,3,1,0:T(8,128)S(1)} fusion(f32[9,8,32,128]{3,2,1,0:T(8,128)S(1)} %copy-done.1, f32[8,32,128]{2,1,0:T(8,128)S(1)} %get-tuple-element.9, f32[32,32]{1,0:T(8,128)S(1)} %copy-done.8), kind=kOutput, calls=%fused_computation.36 | convolution fusion | flops 113541120 | bytes 2494464 | tf_op jit(solution)/shard_map/ab,nzby->nzay/dot_general | solution.py:61
  20.5 0.0 copy-done.11
  20.5 0.0 copy-start.6
  20.5 0.8 convolution_bitcast_fusion
  21.3 18.3 %all_gather.6 = f32[16,9,8,128]{3,2,1,0:T(8,128)S(1)} all-gather(f32[4,9,8,128]{3,2,1,0:T(8,128)S(1)} %copy.63), channel_id=1, replica_groups=mesh['gx'=4,'gy'=4,'gz'=2] {'gx'}, dimensions={0}, use_global_device_ids=true | all-gather | bytes 737280 | tf_op jit(solution)/shard_map/all_gather | solution.py:63
  39.6 0.0 copy-done.6
  39.6 0.0 copy-start.12
  39.6 2.1 %fusion.23 = f32[9,8,32,128]{3,2,1,0:T(8,128)} fusion(f32[9,8,32,128]{3,2,1,0:T(8,128)S(1)} %copy-done.1, f32[8,32,128]{2,1,0:T(8,128)S(1)} %get-tuple-element.8, f32[128,128]{1,0:T(8,128)S(1)} %copy-done), kind=kOutput, calls=%fused_computation.33 | convolution fusion | flops 453279744 | bytes 2555904 | tf_op jit(solution)/shard_map/ab,nzxb->nzxa/dot_general | solution.py:66
  41.8 0.0 copy-done.12
  41.8 4.7 %fusion.21 = f32[9,8,32,4]{2,3,1,0:T(4,128)S(1)} fusion(f32[9,8,32,128]{3,2,1,0:T(8,128)S(1)} %copy-done.1, f32[8,32,128]{2,1,0:T(8,128)S(1)} %get-tuple-element.8, f32[4,128]{1,0:T(4,128)S(1)} %copy-done.12), kind=kOutput, calls=%fused_computation.31 | convolution fusion | flops 14450688 | bytes 1349632 | tf_op jit(solution)/shard_map/kb,nzxb->nzxk/dot_general | solution.py:67
  46.4 11.3 %all_gather.7 = f32[9,8,32,16]{2,1,0,3:T(8,128)S(1)} all-gather(f32[9,8,32,4]{2,1,0,3:T(8,128)S(1)} %copy.65), channel_id=1, replica_groups=mesh['gx'=4,'gy'=4,'gz'=2] {'gy'}, dimensions={3}, use_global_device_ids=true | all-gather | bytes 184320 | tf_op jit(solution)/shard_map/all_gather | solution.py:68
  57.7 0.0 copy-done.13
  57.7 0.5 convolution_bitcast_fusion.1
  58.2 0.0 copy-done.9
  58.2 0.0 copy-start.14
  58.2 0.0 copy-start.16
  58.2 3.2 %fusion.9 = f32[19,8,32,128]{3,0,2,1:T(8,128)S(1)} fusion(f32[9,8,32,128]{3,2,1,0:T(8,128)S(1)} %log.7, s32[19,9]{0,1:T(8,128)S(1)} %copy-done.9), kind=kOutput, calls=%fused_computation.12 | convolution fusion | flops 67240104 | bytes 3670700 | tf_op jit(solution)/shard_map/rn,nzxy->rzxy/dot_general | solution.py:83
  61.4 0.0 copy-done.14
  61.4 1.1 %fusion.28 = f32[9,8,32,4]{2,3,1,0:T(4,128)} fusion(f32[9,8,32,16]{2,1,0,3:T(8,128)S(1)} %all_gather.7, f32[4,16]{1,0:T(4,128)S(1)} %copy-done.14), kind=kOutput, calls=%fused_computation.38 | convolution fusion | flops 1769472 | bytes 184576 | tf_op jit(solution)/shard_map/ij,nzxj->nzxi/dot_general | solution.py:69
  62.6 0.0 copy-start.22
  62.6 2.1 %fusion.20 = f32[9,8,32,128]{3,2,1,0:T(8,128)} fusion(f32[9,8,128,32]{2,3,1,0:T(8,128)S(1)} %fusion.26, f32[4,9,8,128]{3,0,2,1:T(4,128)S(1)} %convolution_bitcast_fusion.1, f32[32,4]{0,1:T(4,128)S(1)} %copy-done.16), kind=kOutput, calls=%fused_computation.25 | convolution fusion | flops 14450688 | bytes 2507264 | tf_op jit(solution)/shard_map/ak,knzy->nzay/dot_general | solution.py:65
  64.7 0.0 copy-start.19
  64.7 0.0 copy-start.7
  64.8 3.3 %fusion.2 = f32[8,32,128,9]{2,3,1,0:T(8,128)S(1)} fusion(f32[19,8,32,128]{3,0,2,1:T(8,128)S(1)} %fusion.9, f32[8,32,128]{2,1,0:T(8,128)S(1)} %get-tuple-element.11, f32[19]{0:T(128)S(1)} %copy-done.20, f32[8,32,128]{2,1,0:T(8,128)S(1)} %get-tuple-element.10, f32[19]{0:T(128)S(1)} %copy-done.21, f32[19]{0:T(128)S(1)} %copy-done.22, s32[19,9]{0,1:T(8,128)S(1)} %copy-done.10), kind=kOutput, calls=%fused_computation.5 | convolution fusion | flops 70353064 | bytes 3933072 | tf_op jit(solution)/shard_map/rn,rzxy->nzxy/dot_general | solution.py:87
  68.1 0.7 convert_element_type.17
  68.7 0.0 collective-permute-done
  68.7 8.6 %scatter_custom_fusion = f32[9,32768]{0,1:T(8,128)} fusion(s32[256]{0:T(256)S(1)} %bitcast.94, f32[]{:T(128)} %constant.6.clone.1, f32[9,256]{0,1:T(8,128)} %collective-permute-done), kind=kCustom, calls=%fused_computation.3 | custom fusion | flops 2304 | bytes 1188868 | tf_op jit(solution)/shard_map/scatter-add | solution.py:92
  77.3 13.3 %scatter_custom_fusion.1 = f32[9,32768]{0,1:T(8,128)} fusion(f32[9,32768]{0,1:T(8,128)} %scatter_custom_fusion, s32[256]{0:T(256)S(1)} %bitcast.93, f32[256,9]{1,0:T(8,128)S(1)} %gather_fusion, f32[256]{0:T(256)S(1)} %bitcast.91), kind=kCustom, calls=%fused_computation.45 | custom fusion | flops 6912 | bytes 1311744 | tf_op jit(solution)/shard_map/scatter-add | solution.py:93
  90.6 10.9 %copy.77 = f32[9,8,32,128]{3,2,1,0:T(8,128)} copy(f32[9,8,32,128]{0,3,2,1:T(8,128)} %bitcast.88) | data formatting | bytes 2359296 | tf_op jit(solution)/shard_map/reshape | solution.py:94
  101.5 4.9 %multiply_add_fusion = (f32[9,8,32,128]{3,2,1,0:T(8,128)}, f32[9,8,32,128]{3,2,1,0:T(8,128)}) fusion(f32[9,8,32,128]{3,2,1,0:T(8,128)S(1)} %copy-done.1, f32[9,8,32,128]{3,2,1,0:T(8,128)} %fusion.20, f32[9,8,32,128]{3,2,1,0:T(8,128)} %fusion.23, f32[9,8,32,4]{2,3,1,0:T(4,128)S(1)} %copy-done.2, f32[128,4]{0,1:T(4,128)S(1)} %copy-done.15, ...), kind=kOutput, calls=%fused_computation.28 | convolution fusion | flops 16809984 | bytes 8558592 | tf_op jit(solution)/shard_map/ak,nzxk->nzxa/dot_general | solution.py:70
  (28 shorter events, 0.1 us)
Async XLA Ops:
  0.6 39.0 %copy-start = (f32[128,128]{1,0:T(8,128)S(1)}, f32[128,128]{1,0:T(8,128)}, u32[]{:S(2)}) copy-start(f32[128,128]{1,0:T(8,128)} %param.34) | copy-start | bytes 196612
  1.4 16.6 %copy-start.17 = (f32[1,1,256]{2,1,0:T(1,128)S(1)}, f32[1,1,256]{2,1,0:T(1,128)}, u32[]{:S(2)}) copy-start(f32[1,1,256]{2,1,0:T(1,128)} %param.46) | copy-start | bytes 3076
  1.4 16.6 %copy-start.18 = (s32[1,1,256]{2,1,0:T(1,128)S(1)}, s32[1,1,256]{2,1,0:T(1,128)}, u32[]{:S(2)}) copy-start(s32[1,1,256]{2,1,0:T(1,128)} %param.45) | copy-start | bytes 3076
  1.4 17.3 %copy-start.1 = (f32[9,8,32,128]{3,2,1,0:T(8,128)S(1)}, f32[9,8,32,128]{3,2,1,0:T(8,128)}, u32[]{:S(2)}) copy-start(f32[9,8,32,128]{3,2,1,0:T(8,128)} %param.24) | copy-start | bytes 3538948
  18.1 1.0 copy-start.3
  18.1 1.0 copy-start.4
  18.1 1.1 %copy-start.5 = (f32[2,8,32,128]{3,2,1,0:T(8,128)S(1)}, f32[2,8,32,128]{3,2,1,0:T(8,128)}, u32[]{:S(2)}) copy-start(f32[2,8,32,128]{3,2,1,0:T(8,128)} %param.25) | copy-start | bytes 786436
  18.2 1.1 %copy-start.8 = (f32[32,32]{1,0:T(8,128)S(1)}, f32[32,32]{1,0:T(8,128)}, u32[]{:S(2)}) copy-start(f32[32,32]{1,0:T(8,128)} %param.30) | copy-start | bytes 12292
  18.2 50.6 %collective-permute-start = (f32[9,256]{0,1:T(8,128)S(1)}, f32[9,256]{0,1:T(8,128)}, u32[]{:S(2)}, u32[]{:S(2)}) collective-permute-start(f32[9,256]{0,1:T(8,128)S(1)} %multiply_bitcast_fusion), channel_id=1, source_target_pairs={{0,1},{1,0},{2,3},{3,2},{4,5},{5,4},{6,7},{7,6},{8,9},{9,8},{10,11... | collective-permute-start | bytes 27656 | tf_op jit(solution)/shard_map/ppermute | solution.py:12
  19.3 1.2 %copy-start.11 = (f32[4,32]{1,0:T(4,128)S(1)}, f32[4,32]{1,0:T(4,128)}, u32[]{:S(2)}) copy-start(f32[4,32]{1,0:T(4,128)} %param.31) | copy-start | bytes 1540
  20.5 19.1 %copy-start.6 = (f32[8,32,128]{2,1,0:T(8,128)S(1)}, f32[8,32,128]{2,1,0:T(8,128)}, u32[]{:S(2)}) copy-start(f32[8,32,128]{2,1,0:T(8,128)} %param.29) | copy-start | bytes 393220
  39.6 2.1 %copy-start.12 = (f32[4,128]{1,0:T(4,128)S(1)}, f32[4,128]{1,0:T(4,128)}, u32[]{:S(2)}) copy-start(f32[4,128]{1,0:T(4,128)} %param.35) | copy-start | bytes 6148
  41.8 15.9 %copy-start.13 = (f32[4,16]{1,0:T(4,128)S(1)}, f32[4,16]{1,0:T(4,128)}, u32[]{:S(2)}) copy-start(f32[4,16]{1,0:T(4,128)} %param.33) | copy-start | bytes 772
  46.4 11.8 %copy-start.9 = (s32[19,9]{0,1:T(8,128)S(1)}, s32[19,9]{0,1:T(8,128)}, u32[]{:S(2)}) copy-start(s32[19,9]{0,1:T(8,128)} %param.41) | copy-start | bytes 2056
  58.2 3.2 %copy-start.14 = (f32[4,16]{1,0:T(4,128)S(1)}, f32[4,16]{1,0:T(4,128)}, u32[]{:S(2)}) copy-start(f32[4,16]{1,0:T(4,128)} %param.37) | copy-start | bytes 772
  58.2 4.4 %copy-start.16 = (f32[32,4]{0,1:T(4,128)S(1)}, f32[32,4]{0,1:T(4,128)}, u32[]{:S(2)}) copy-start(f32[32,4]{0,1:T(4,128)} %param.32) | copy-start | bytes 1540
  62.6 2.2 %copy-start.10 = (s32[19,9]{0,1:T(8,128)S(1)}, s32[19,9]{0,1:T(8,128)}, u32[]{:S(2)}) copy-start(s32[19,9]{0,1:T(8,128)} %param.42) | copy-start | bytes 2056
  62.6 2.2 %copy-start.20 = (f32[19]{0:T(128)S(1)}, f32[19]{0:T(128)}, u32[]{:S(2)}) copy-start(f32[19]{0:T(128)} %param.40) | copy-start | bytes 232
  62.6 2.2 %copy-start.21 = (f32[19]{0:T(128)S(1)}, f32[19]{0:T(128)}, u32[]{:S(2)}) copy-start(f32[19]{0:T(128)} %param.39) | copy-start | bytes 232
  62.6 2.2 %copy-start.22 = (f32[19]{0:T(128)S(1)}, f32[19]{0:T(128)}, u32[]{:S(2)}) copy-start(f32[19]{0:T(128)} %param.38) | copy-start | bytes 232
  64.7 3.3 %copy-start.19 = (s32[1,1,256]{2,1,0:T(1,128)S(1)}, s32[1,1,256]{2,1,0:T(1,128)}, u32[]{:S(2)}) copy-start(s32[1,1,256]{2,1,0:T(1,128)} %param.44) | copy-start | bytes 3076
  64.7 3.3 %copy-start.7 = (s32[8,32,128]{2,1,0:T(8,128)S(1)}, s32[8,32,128]{2,1,0:T(8,128)}, u32[]{:S(2)}) copy-start(s32[8,32,128]{2,1,0:T(8,128)} %param.47) | copy-start | bytes 393220
  90.6 10.9 %copy-start.2 = (f32[9,8,32,4]{2,3,1,0:T(4,128)S(1)}, f32[9,8,32,4]{2,3,1,0:T(4,128)}, u32[]{:S(2)}) copy-start(f32[9,8,32,4]{2,3,1,0:T(4,128)} %fusion.28) | copy-start | bytes 110596
  90.6 10.9 %copy-start.15 = (f32[128,4]{0,1:T(4,128)S(1)}, f32[128,4]{0,1:T(4,128)}, u32[]{:S(2)}) copy-start(f32[128,4]{0,1:T(4,128)} %param.36) | copy-start | bytes 6148
where the time goes:
time: 107 us; the launch traced here: 106 us
  blocking collectives  29.5 us (28%)
  local copies, waits for them, and re-layouts  28.2 us (26%)
  matrix products  23.8 us (22%)
  other arithmetic  23.5 us (22%)
    all_gather x1, blocking collectives, per_device(): whole_x = lax.all_gather(side_x, 'gx', axis=0, tiled=True)  18.3 us
    scatter-add x1, other arithmetic, per_device(): wall = wall.at[:, source_cells].add(-outgoing)  13.3 us
    all_gather x1, blocking collectives, per_device(): whole_y = lax.all_gather(side_y, 'gy', axis=3, tiled=True)  11.3 us
    reshape x1, local copies, waits for them, and re-layouts, per_device(): wall = wall.reshape(species_partial_mass.shape)  10.9 us
    unnamed x47, local copies, waits for them, and re-layouts  10.6 us
    scatter-add x1, other arithmetic, per_device(): wall = wall.at[:, target_cells].add(incoming)  8.55 us
    gather x1, local copies, waits for them, and re-layouts, per_device(): outgoing = flat[:, source_cells] * weight[None, :]  6.49 us
    dot_general x1, matrix products, per_device(): jnp.einsum('ak,nzxk->nzxa', second_dir_border_spread, solved_y, precision...  4.94 us
  transfers between devices with their start and end apart: 1, of which 0 were waited for; matrix products, arithmetic and copies ran while one was open for 19% of the time, Pallas kernels for 0%

commit v1 on v0

v1 whole, which is shorter than its diff:
```python
import functools

import jax
import jax.numpy as jnp
from jax import lax
from jax.experimental import pallas as pl
from jax.experimental.pallas import tpu as pltpu
from jax.sharding import PartitionSpec as P

HI = lax.Precision.HIGHEST
F32 = jnp.float32
B16 = jnp.bfloat16
MESH = pl.DeviceIdType.MESH
LANES = 128


def shift_of(n):
    assert n & (n - 1) == 0
    return n.bit_length() - 1


def over(value, n):
    return lax.shift_right_logical(value, jnp.int32(shift_of(n)))


def rest(value, n):
    return value & (n - 1)


def iota(shape, dim):
    return lax.broadcasted_iota(jnp.int32, shape, dim)


def ones_where(mask):
    return jnp.where(mask, F32(1), F32(0))


def fdot(a, b):
    return jnp.dot(a, b, precision=HI, preferred_element_type=F32)


def bdot(a, b):
    return jnp.dot(a, b, preferred_element_type=F32)


def split(value):
    high = value.astype(B16)
    return high, (value - high.astype(F32)).astype(B16)


def dot3(a, b):
    return bdot(a[0], b[0]) + bdot(a[0], b[1]) + bdot(a[1], b[0])


def dot2(a, b):
    return bdot(a, b[0]) + bdot(a, b[1])


def kernel(
    n_gx,
    n_gy,
    rows_x,
    sp,
    motion,
    g_main,
    g_cross,
    vol,
    kelvin,
    dx,
    cx,
    bx,
    mx,
    dy,
    cy,
    by,
    my,
    ln_ref,
    kexp,
    energy,
    flags,
    stoich,
    supply,
    target,
    used,
    weight,
    q,
    ex_all,
    ey_all,
    wall_out,
    wall_in,
    fx_h,
    fx_l,
    fy_h,
    fy_l,
    u_h,
    u_l,
    acc,
    x_send,
    x_recv,
    y_send,
    y_recv,
    w_send,
    w_recv,
):
    species, rows, lanes = sp.shape
    planes = rows // rows_x
    unknowns = cx.shape[0]
    slots = supply.shape[1]
    reactions = flags.shape[0]
    padded = ey_all.shape[1]
    me_x, me_y, me_z = lax.axis_index("gx"), lax.axis_index("gy"), lax.axis_index("gz")

    def along_x(d):
        return {"gx": lax.rem(me_x + d, n_gx)}

    def along_y(d):
        return {"gy": lax.rem(me_y + d, n_gy)}

    across = {"gz": 1 - me_z}

    barrier = pltpu.get_barrier_semaphore()
    for d in range(1, n_gx):
        pl.semaphore_signal(barrier, inc=1, device_id=along_x(d), device_id_type=MESH)
    for d in range(1, n_gy):
        pl.semaphore_signal(barrier, inc=1, device_id=along_y(d), device_id_type=MESH)
    pl.semaphore_signal(barrier, inc=1, device_id=across, device_id_type=MESH)

    def part(s):
        return slice(s * lanes, (s + 1) * lanes)

    contra_x = g_main[0] * motion[0] + g_cross[0] * motion[1]
    for s in range(species):
        fx_h[:, part(s)], fx_l[:, part(s)] = split(contra_x * sp[s])
    pick = ones_where(rest(iota((rows, rows_x), 0), rows_x) == iota((rows, rows_x), 1))
    pick_t = ones_where(rest(iota((rows_x, rows), 1), rows_x) == iota((rows_x, rows), 0))
    side = unknowns * planes
    sel = ones_where(over(iota((side, unknowns), 0), planes) == iota((side, unknowns), 1))
    cx_big = jnp.where(
        rest(iota((side, rows), 0), planes) == over(iota((side, rows), 1), rows_x),
        fdot(fdot(sel, cx[...]), pick_t),
        F32(0),
    )
    ex_all[me_x] = dot3(split(cx_big), (fx_h[...], fx_l[...]))
    pl.semaphore_wait(barrier, n_gx + n_gy - 1)
    x_copies = []
    for d in range(1, n_gx):
        copy = pltpu.make_async_remote_copy(
            src_ref=ex_all.at[me_x],
            dst_ref=ex_all.at[me_x],
            send_sem=x_send.at[d],
            recv_sem=x_recv.at[d],
            device_id=along_x(d),
            device_id_type=MESH,
        )
        copy.start()
        x_copies.append(copy)

    contra_y = g_cross[1] * motion[0] + g_main[1] * motion[1]
    for s in range(species):
        fy_h[:, part(s)], fy_l[:, part(s)] = split(contra_y * sp[s])
    sel = ones_where(rest(iota((lanes, unknowns), 0), unknowns) == iota((lanes, unknowns), 1))
    cy_t = fdot(sel, cy[...]).T
    owner = over(iota((lanes, lanes), 1), unknowns)
    cy_h, cy_l = split(
        jnp.concatenate([jnp.where(owner == s, cy_t, F32(0)) for s in range(species)], axis=0)
    )
    ey = dot3((fy_h[...], fy_l[...]), (cy_h, cy_l))
    ey_all[me_y] = ey.T[:padded]
    y_copies = []
    for d in range(1, n_gy):
        copy = pltpu.make_async_remote_copy(
            src_ref=ey_all.at[me_y],
            dst_ref=ey_all.at[me_y],
            send_sem=y_send.at[d],
            recv_sem=y_recv.at[d],
            device_id=along_y(d),
            device_id_type=MESH,
        )
        copy.start()
        y_copies.append(copy)

    def down(row):
        return jnp.broadcast_to(row, (lanes, slots)).T

    supply_col = down(supply[...])
    carried = down(weight[...] * used[...].astype(F32))
    wide = jnp.concatenate([over(supply_col, lanes)] * (rows // lanes), axis=1)
    from_rows = ones_where(wide == iota((slots, rows), 1)).astype(B16)
    from_lane = rest(supply_col, lanes) == iota((slots, lanes), 1)
    for s in range(species):
        u_h[:, part(s)], u_l[:, part(s)] = split(sp[s])
    gathered = dot2(from_rows, (u_h[...], u_l[...]))
    lane = iota((slots, lanes), 1)
    sent = jnp.zeros((slots, lanes), F32)
    for s in range(species):
        kept = jnp.where(from_lane, gathered[:, part(s)] * carried, F32(0))
        u_h[:, part(s)], u_l[:, part(s)] = split(-kept)
        sent = jnp.where(lane == s, jnp.sum(kept, axis=1, keepdims=True), sent)
    wall_out[...] = sent
    w_copy = pltpu.make_async_remote_copy(
        src_ref=wall_out,
        dst_ref=wall_in,
        send_sem=w_send,
        recv_sem=w_recv,
        device_id=across,
        device_id_type=MESH,
    )
    w_copy.start()

    chunk = 16

    def chemistry(i, carry):
        at = pl.ds(pl.multiple_of(i * chunk, chunk), chunk)
        temperature = kelvin[at, :]
        ln_t = jnp.log(temperature / F32(1500.0))
        rec_t = F32(1.0) / temperature - F32(1.0 / 1500.0)
        logs = [jnp.log(sp[s, at, :]) for s in range(species)]
        sums = [jnp.zeros((chunk, lanes), F32) for _ in range(species)]
        for r in range(reactions):
            value = ln_ref[r] + kexp[r] * ln_t - energy[r] * rec_t
            for s in range(species):
                value = value + flags[r, s].astype(F32) * logs[s]
            progress = jnp.exp(value)
            for s in range(species):
                sums[s] = sums[s] + stoich[r, s].astype(F32) * progress
        for s in range(species):
            q[s, at, :] = F32(0.2) * sums[s]
        return carry

    lax.fori_loop(0, rows // chunk, chemistry, 0)

    same = over(iota((rows, rows), 0), rows_x) == over(iota((rows, rows), 1), rows_x)
    dx_big = jnp.where(same, fdot(fdot(pick, dx[...]), pick_t), F32(0))
    acc[...] = dot3(split(dx_big), (fx_h[...], fx_l[...]))
    dy_t = split(dy[...].T)
    for s in range(species):
        acc[:, part(s)] += dot3((fy_h[:, part(s)], fy_l[:, part(s)]), dy_t)

    to_supply = ones_where(
        over(jnp.broadcast_to(supply[...], (rows, slots)), lanes) == iota((rows, slots), 0)
    ).astype(B16)
    to_target = ones_where(
        over(jnp.broadcast_to(target[...], (rows, slots)), lanes) == iota((rows, slots), 0)
    ).astype(B16)
    own_wall = dot2(to_supply, (u_h[...], u_l[...]))
    for s in range(species):
        q[s] += own_wall[:, part(s)]
    to_lane = rest(down(target[...]), lanes) == lane
    w_copy.wait_recv()
    incoming = wall_in[...]
    for s in range(species):
        spread = jnp.broadcast_to(incoming[:, s : s + 1], (slots, lanes))
        u_h[:, part(s)], u_l[:, part(s)] = split(jnp.where(to_lane, spread, F32(0)))
    far_wall = dot2(to_target, (u_h[...], u_l[...]))
    for s in range(species):
        q[s] += far_wall[:, part(s)]

    wy = fdot(by[...], my[...])
    pieces = []
    for i in range(n_gy):
        shape = (padded, n_gy * unknowns)
        sel = ones_where(rest(iota(shape, 0), unknowns) + i * unknowns == iota(shape, 1))
        pieces.append(
            lax.dot_general(
                sel, wy, (((1,), (1,)), ((), ())), precision=HI, preferred_element_type=F32
            )
        )
    base = jnp.concatenate(pieces, axis=0)
    owner = jnp.concatenate([over(iota((padded, lanes), 0), unknowns)] * n_gy, axis=0)
    wy_big = jnp.concatenate(
        [jnp.where(owner == s, base, F32(0)) for s in range(species)], axis=1
    )
    for copy in y_copies:
        copy.wait_recv()
    ey = ey_all[...].reshape(n_gy * padded, rows).T
    acc[...] += dot3(split(ey), split(wy_big))

    count = n_gx * unknowns
    wide = count * planes
    sel = ones_where(over(iota((count, wide), 1), planes) == iota((count, wide), 0))
    wx = fdot(pick, fdot(fdot(bx[...], mx[...]), sel))
    wx_big = split(
        jnp.where(
            over(iota((rows, wide), 0), rows_x) == rest(iota((rows, wide), 1), planes), wx, F32(0)
        )
    )
    for copy in x_copies:
        copy.wait_recv()
    ex = split(ex_all[...].reshape(wide, species * lanes))
    total = acc[...] + dot3(wx_big, ex)
    for s in range(species):
        q[s] = q[s] - vol[...] * total[:, part(s)]

    for copy in x_copies + y_copies + [w_copy]:
        copy.wait_send()


def per_device(n_gx, n_gy, *args):
    species_partial_mass = args[0]
    open_volume_flags = args[-1]
    species, planes, rows_x, lanes = species_partial_mass.shape
    rows = planes * rows_x
    ins = [
        species_partial_mass.reshape(species, rows, lanes),
        *(a.reshape(2, rows, lanes) for a in args[1:4]),
        *(a.reshape(rows, lanes) for a in args[4:6]),
        *args[6:19],
        *(a.reshape(1, -1) for a in args[19:23]),
    ]
    slots = ins[-1].shape[1]
    unknowns = args[7].shape[0]
    padded = -(-species * unknowns // 16) * 16
    wide = species * lanes
    vmem = pl.BlockSpec(memory_space=pltpu.VMEM)
    smem = pl.BlockSpec(memory_space=pltpu.SMEM)
    q = pl.pallas_call(
        functools.partial(kernel, n_gx, n_gy, rows_x),
        out_shape=jax.ShapeDtypeStruct((species, rows, lanes), F32),
        in_specs=[vmem] * 14 + [smem] * 5 + [vmem] * 4,
        out_specs=vmem,
        scratch_shapes=[
            pltpu.VMEM((n_gx, unknowns * planes, wide), F32),
            pltpu.VMEM((n_gy, padded, rows), F32),
            pltpu.VMEM((slots, lanes), F32),
            pltpu.VMEM((slots, lanes), F32),
            *([pltpu.VMEM((rows, wide), B16)] * 4),
            *([pltpu.VMEM((max(rows, slots), wide), B16)] * 2),
            pltpu.VMEM((rows, wide), F32),
            pltpu.SemaphoreType.DMA((n_gx,)),
            pltpu.SemaphoreType.DMA((n_gx,)),
            pltpu.SemaphoreType.DMA((n_gy,)),
            pltpu.SemaphoreType.DMA((n_gy,)),
            pltpu.SemaphoreType.DMA,
            pltpu.SemaphoreType.DMA,
        ],
        compiler_params=pltpu.CompilerParams(
            collective_id=0, has_side_effects=True, vmem_limit_bytes=48 * 2**20
        ),
    )(*ins)
    q = q.reshape(species_partial_mass.shape)
    section_rhs = open_volume_flags.astype(F32)[None] * q
    section_state = species_partial_mass + 0.25 * section_rhs
    return (section_rhs, section_state)


def solution(mesh):
    grid = P(None, "gz", "gx", "gy")
    cells = P("gz", "gx", "gy")
    faces = P("gx", "gy", "gz")
    in_specs = (
        *([grid] * 4),
        *([cells] * 2),
        *([P()] * 3),
        P("gx", None),
        *([P()] * 3),
        P("gy", None),
        *([P()] * 5),
        *([faces] * 4),
        cells,
    )
    return jax.shard_map(
        functools.partial(per_device, mesh.shape["gx"], mesh.shape["gy"]),
        mesh=mesh,
        in_specs=in_specs,
        out_specs=(grid, grid),
        check_vma=False,
    )
```

time: 107 us -> 41.5 us (0.39)
  blocking collectives: 29.5 us -> 0 us
  matrix products: 23.8 us -> 0 us
  other arithmetic: 23.5 us -> 2.64 us
  Pallas kernels: 0 us -> 19.4 us
  local copies, waits for them, and re-layouts: 28.2 us -> 18 us
    all_gather x2 -> x0, blocking collectives: 29.5 us -> none  [the longest x1 18.3 us: per_device(): whole_x = lax.all_gather(side_x, 'gx', axis=0, tiled=True)]
    dot_general x10 -> x0, matrix products: 23.8 us -> none  [the longest x1 4.94 us: per_device(): jnp.einsum('ak,nzxk->nzxa', second_dir_border_spread, solved_y, precision...]
    scatter-add x2 -> x0, other arithmetic: 21.9 us -> none  [the longest x1 13.3 us: per_device(): wall = wall.at[:, source_cells].add(-outgoing)]
    pallas_call x0 -> x1, Pallas kernels: none -> 19.4 us  [per_device(): pl.pallas_call(functools.partial(kernel, n_gx, n_gy, rows_x), out_shape=j...]
    reshape x1 -> x0, local copies, waits for them, and re-layouts: 10.9 us -> none  [per_device(): wall = wall.reshape(species_partial_mass.shape)]
    unnamed x47 -> x42, local copies, waits for them, and re-layouts: 10.6 us -> 18 us
    gather x1 -> x0, local copies, waits for them, and re-layouts: 6.49 us -> none  [per_device(): outgoing = flat[:, source_cells] * weight[None, :]]
    add x0 -> x1, other arithmetic: none -> 1.73 us  [per_device(): section_state = species_partial_mass + 0.25 * section_rhs]
  transfers between devices with their start and end apart: 1 -> 0, of which waited for: 0 -> 0; matrix products, arithmetic and copies ran while one was open for 19% -> 0% of each run, Pallas kernels for 0% -> 0%
where the time goes in v1:
time: 41.5 us; the launch traced here: 40.8 us
  Pallas kernels  19.4 us (47%)
  local copies, waits for them, and re-layouts  18 us (43%)
  other arithmetic  2.64 us (6%)
  between operations  0.67 us (2%)
    pallas_call x1, Pallas kernels, per_device(): pl.pallas_call(functools.partial(kernel, n_gx, n_gy, rows_x), out_shape=j...  19.4 us
    unnamed x42, local copies, waits for them, and re-layouts  18 us
    add x1, other arithmetic, per_device(): section_state = species_partial_mass + 0.25 * section_rhs  1.73 us
    convert_element_type x1, other arithmetic, per_device(): section_rhs = open_volume_flags.astype(F32)[None] * q  0.91 us

profile of v1, /device:TPU:0, one launch (start us, length us, event | category | flops | bytes accessed | tf_op | source)
XLA Modules:
  0.0 40.8 jit_solution(4619769574367254037)
XLA Ops:
  0.6 0.8 %copy.28.flags = s32[19,9]{1,0:T(8,128)S(1)} copy(s32[19,9]{0,1:T(8,128)} %param.41) | data formatting | bytes 1368 | tf_op args[17]
  1.4 0.8 %copy.29.stoich = s32[19,9]{1,0:T(8,128)S(1)} copy(s32[19,9]{0,1:T(8,128)} %param.42) | data formatting | bytes 1368 | tf_op args[18]
  2.2 0.8 %copy.26.bx = f32[32,4]{1,0:T(8,128)S(1)} copy(f32[32,4]{0,1:T(4,128)} %param.32) | data formatting | bytes 1024 | tf_op args[8]
  3.0 0.8 %copy.27.by = f32[128,4]{1,0:T(8,128)S(1)} copy(f32[128,4]{0,1:T(4,128)} %param.36) | data formatting | bytes 4096 | tf_op args[12]
  3.7 0.9 %convert_element_type.3 = f32[8,32,128]{2,1,0:T(8,128)S(1)} convert(s32[8,32,128]{2,1,0:T(8,128)} %param.47) | non-fusion elementwise | flops 32768 | bytes 262144 | tf_op jit(solution)/shard_map/convert_element_type | solution.py:341
  4.7 0.0 copy-start
  4.7 1.3 %copy-done = f32[9,8,32,128]{3,2,1,0:T(8,128)S(1)} copy-done((f32[9,8,32,128]{3,2,1,0:T(8,128)S(1)}, f32[9,8,32,128]{3,2,1,0:T(8,128)}, u32[]{:S(2)}) %copy-start) | copy-done | bytes 1179672
  5.9 0.0 copy-start.1
  5.9 0.9 %copy-done.1 = f32[2,8,32,128]{3,2,1,0:T(8,128)S(1)} copy-done((f32[2,8,32,128]{3,2,1,0:T(8,128)S(1)}, f32[2,8,32,128]{3,2,1,0:T(8,128)}, u32[]{:S(2)}) %copy-start.1) | copy-done | bytes 262168
  6.9 0.0 copy-start.2
  6.9 0.9 %copy-done.2 = f32[2,8,32,128]{3,2,1,0:T(8,128)S(1)} copy-done((f32[2,8,32,128]{3,2,1,0:T(8,128)S(1)}, f32[2,8,32,128]{3,2,1,0:T(8,128)}, u32[]{:S(2)}) %copy-start.2) | copy-done | bytes 262168
  7.8 0.0 copy-start.3
  7.8 0.9 %copy-done.3 = f32[2,8,32,128]{3,2,1,0:T(8,128)S(1)} copy-done((f32[2,8,32,128]{3,2,1,0:T(8,128)S(1)}, f32[2,8,32,128]{3,2,1,0:T(8,128)}, u32[]{:S(2)}) %copy-start.3) | copy-done | bytes 262168
  8.8 0.0 copy-start.4
  8.8 0.9 %copy-done.4 = f32[8,32,128]{2,1,0:T(8,128)S(1)} copy-done((f32[8,32,128]{2,1,0:T(8,128)S(1)}, f32[8,32,128]{2,1,0:T(8,128)}, u32[]{:S(2)}) %copy-start.4) | copy-done | bytes 131096
  9.7 0.0 copy-start.5
  9.7 0.9 %copy-done.5 = f32[8,32,128]{2,1,0:T(8,128)S(1)} copy-done((f32[8,32,128]{2,1,0:T(8,128)S(1)}, f32[8,32,128]{2,1,0:T(8,128)}, u32[]{:S(2)}) %copy-start.5) | copy-done | bytes 131096
  10.6 0.0 copy-start.6
  10.6 0.8 %copy-done.6 = f32[128,128]{1,0:T(8,128)S(1)} copy-done((f32[128,128]{1,0:T(8,128)S(1)}, f32[128,128]{1,0:T(8,128)}, u32[]{:S(2)}) %copy-start.6) | copy-done | bytes 65560
  11.4 0.0 copy-start.7
  11.4 0.7 %copy-done.7 = f32[32,32]{1,0:T(8,128)S(1)} copy-done((f32[32,32]{1,0:T(8,128)S(1)}, f32[32,32]{1,0:T(8,128)}, u32[]{:S(2)}) %copy-start.7) | copy-done | bytes 4120
  12.2 0.0 copy-start.8
  12.2 0.7 %copy-done.8 = f32[4,32]{1,0:T(4,128)S(1)} copy-done((f32[4,32]{1,0:T(4,128)S(1)}, f32[4,32]{1,0:T(4,128)}, u32[]{:S(2)}) %copy-start.8) | copy-done | bytes 536
  12.8 0.0 copy-start.9
  12.8 0.7 %copy-done.9 = f32[4,16]{1,0:T(4,128)S(1)} copy-done((f32[4,16]{1,0:T(4,128)S(1)}, f32[4,16]{1,0:T(4,128)}, u32[]{:S(2)}) %copy-start.9) | copy-done | bytes 280
  13.5 0.0 copy-start.10
  13.5 0.7 %copy-done.10 = f32[4,128]{1,0:T(4,128)S(1)} copy-done((f32[4,128]{1,0:T(4,128)S(1)}, f32[4,128]{1,0:T(4,128)}, u32[]{:S(2)}) %copy-start.10) | copy-done | bytes 2072
  14.2 0.0 copy-start.11
  14.2 0.7 %copy-done.11 = f32[4,16]{1,0:T(4,128)S(1)} copy-done((f32[4,16]{1,0:T(4,128)S(1)}, f32[4,16]{1,0:T(4,128)}, u32[]{:S(2)}) %copy-start.11) | copy-done | bytes 280
  14.9 0.0 copy-start.12
  14.9 0.7 %copy-done.12 = s32[1,1,256]{2,1,0:T(1,128)S(1)} copy-done((s32[1,1,256]{2,1,0:T(1,128)S(1)}, s32[1,1,256]{2,1,0:T(1,128)}, u32[]{:S(2)}) %copy-start.12) | copy-done | bytes 1048
  15.6 0.0 copy-start.13
  15.6 0.7 %copy-done.13 = s32[1,1,256]{2,1,0:T(1,128)S(1)} copy-done((s32[1,1,256]{2,1,0:T(1,128)S(1)}, s32[1,1,256]{2,1,0:T(1,128)}, u32[]{:S(2)}) %copy-start.13) | copy-done | bytes 1048
  16.2 0.0 copy-start.14
  16.2 0.7 %copy-done.14 = s32[1,1,256]{2,1,0:T(1,128)S(1)} copy-done((s32[1,1,256]{2,1,0:T(1,128)S(1)}, s32[1,1,256]{2,1,0:T(1,128)}, u32[]{:S(2)}) %copy-start.14) | copy-done | bytes 1048
  16.9 0.0 copy-start.15
  16.9 0.7 %copy-done.15 = f32[1,1,256]{2,1,0:T(1,128)S(1)} copy-done((f32[1,1,256]{2,1,0:T(1,128)S(1)}, f32[1,1,256]{2,1,0:T(1,128)}, u32[]{:S(2)}) %copy-start.15) | copy-done | bytes 1048
  17.6 0.0 copy-start.16
  17.6 0.7 %copy-done.16 = f32[19]{0:T(128)S(1)} copy-done((f32[19]{0:T(128)S(1)}, f32[19]{0:T(128)}, u32[]{:S(2)}) %copy-start.16) | copy-done | bytes 100
  18.3 0.0 copy-start.17
  18.3 0.7 %copy-done.17 = f32[19]{0:T(128)S(1)} copy-done((f32[19]{0:T(128)S(1)}, f32[19]{0:T(128)}, u32[]{:S(2)}) %copy-start.17) | copy-done | bytes 100
  18.9 0.0 copy-start.18
  18.9 0.7 %copy-done.18 = f32[19]{0:T(128)S(1)} copy-done((f32[19]{0:T(128)S(1)}, f32[19]{0:T(128)}, u32[]{:S(2)}) %copy-start.18) | copy-done | bytes 100
  19.6 19.4 %shard_map.239 = f32[9,256,128]{2,1,0:T(8,128)S(1)} custom-call(f32[9,256,128]{2,1,0:T(8,128)S(1)} %bitcast.11, f32[2,256,128]{2,1,0:T(8,128)S(1)} %bitcast.13, f32[2,256,128]{2,1,0:T(8,128)S(1)} %bitcast.14, f32[2,256,128]{2,1,0:T(8,128)S(1)} %bitcast.15, f32[256,128]{1,0:T(8,128)S(1)} %bitcast.16, f32[256,128]{1,0:T(8,128)S(1)} %bitcast.17, ...), custom_call_target="tpu_custom_call" | custom-call | tf_op jit(solution)/shard_map/pallas_call | solution.py:316
  39.0 1.7 %multiply_add_fusion = (f32[9,8,32,128]{3,2,1,0:T(8,128)}, f32[9,8,32,128]{3,2,1,0:T(8,128)}) fusion(f32[9,8,32,128]{3,2,1,0:T(8,128)S(1)} %copy-done, f32[9,8,32,128]{3,2,1,0:T(8,128)S(1)} %bitcast.12, f32[8,32,128]{2,1,0:T(8,128)S(1)} %convert_element_type.3), kind=kLoop, calls=%fused_computation | loop fusion | flops 884736 | bytes 4849664 | tf_op jit(solution)/shard_map/add | solution.py:342
Async XLA Ops:
  4.7 1.3 %copy-start = (f32[9,8,32,128]{3,2,1,0:T(8,128)S(1)}, f32[9,8,32,128]{3,2,1,0:T(8,128)}, u32[]{:S(2)}) copy-start(f32[9,8,32,128]{3,2,1,0:T(8,128)} %param.24) | copy-start | bytes 3538948
  5.9 0.9 %copy-start.1 = (f32[2,8,32,128]{3,2,1,0:T(8,128)S(1)}, f32[2,8,32,128]{3,2,1,0:T(8,128)}, u32[]{:S(2)}) copy-start(f32[2,8,32,128]{3,2,1,0:T(8,128)} %param.25) | copy-start | bytes 786436
  6.9 0.9 %copy-start.2 = (f32[2,8,32,128]{3,2,1,0:T(8,128)S(1)}, f32[2,8,32,128]{3,2,1,0:T(8,128)}, u32[]{:S(2)}) copy-start(f32[2,8,32,128]{3,2,1,0:T(8,128)} %param.26) | copy-start | bytes 786436
  7.8 0.9 %copy-start.3 = (f32[2,8,32,128]{3,2,1,0:T(8,128)S(1)}, f32[2,8,32,128]{3,2,1,0:T(8,128)}, u32[]{:S(2)}) copy-start(f32[2,8,32,128]{3,2,1,0:T(8,128)} %param.27) | copy-start | bytes 786436
  8.8 0.9 %copy-start.4 = (f32[8,32,128]{2,1,0:T(8,128)S(1)}, f32[8,32,128]{2,1,0:T(8,128)}, u32[]{:S(2)}) copy-start(f32[8,32,128]{2,1,0:T(8,128)} %param.28) | copy-start | bytes 393220
  9.7 0.9 %copy-start.5 = (f32[8,32,128]{2,1,0:T(8,128)S(1)}, f32[8,32,128]{2,1,0:T(8,128)}, u32[]{:S(2)}) copy-start(f32[8,32,128]{2,1,0:T(8,128)} %param.29) | copy-start | bytes 393220
  10.6 0.8 %copy-start.6 = (f32[128,128]{1,0:T(8,128)S(1)}, f32[128,128]{1,0:T(8,128)}, u32[]{:S(2)}) copy-start(f32[128,128]{1,0:T(8,128)} %dy.1) | copy-start | bytes 196612
  11.4 0.7 %copy-start.7 = (f32[32,32]{1,0:T(8,128)S(1)}, f32[32,32]{1,0:T(8,128)}, u32[]{:S(2)}) copy-start(f32[32,32]{1,0:T(8,128)} %dx.1) | copy-start | bytes 12292
  12.2 0.7 %copy-start.8 = (f32[4,32]{1,0:T(4,128)S(1)}, f32[4,32]{1,0:T(4,128)}, u32[]{:S(2)}) copy-start(f32[4,32]{1,0:T(4,128)} %cx.1) | copy-start | bytes 1540
  12.8 0.7 %copy-start.9 = (f32[4,16]{1,0:T(4,128)S(1)}, f32[4,16]{1,0:T(4,128)}, u32[]{:S(2)}) copy-start(f32[4,16]{1,0:T(4,128)} %mx.1) | copy-start | bytes 772
  13.5 0.7 %copy-start.10 = (f32[4,128]{1,0:T(4,128)S(1)}, f32[4,128]{1,0:T(4,128)}, u32[]{:S(2)}) copy-start(f32[4,128]{1,0:T(4,128)} %cy.1) | copy-start | bytes 6148
  14.2 0.7 %copy-start.11 = (f32[4,16]{1,0:T(4,128)S(1)}, f32[4,16]{1,0:T(4,128)}, u32[]{:S(2)}) copy-start(f32[4,16]{1,0:T(4,128)} %my.1) | copy-start | bytes 772
  14.9 0.7 %copy-start.12 = (s32[1,1,256]{2,1,0:T(1,128)S(1)}, s32[1,1,256]{2,1,0:T(1,128)}, u32[]{:S(2)}) copy-start(s32[1,1,256]{2,1,0:T(1,128)} %param.43) | copy-start | bytes 3076
  15.6 0.7 %copy-start.13 = (s32[1,1,256]{2,1,0:T(1,128)S(1)}, s32[1,1,256]{2,1,0:T(1,128)}, u32[]{:S(2)}) copy-start(s32[1,1,256]{2,1,0:T(1,128)} %param.44) | copy-start | bytes 3076
  16.2 0.7 %copy-start.14 = (s32[1,1,256]{2,1,0:T(1,128)S(1)}, s32[1,1,256]{2,1,0:T(1,128)}, u32[]{:S(2)}) copy-start(s32[1,1,256]{2,1,0:T(1,128)} %param.45) | copy-start | bytes 3076
  16.9 0.7 %copy-start.15 = (f32[1,1,256]{2,1,0:T(1,128)S(1)}, f32[1,1,256]{2,1,0:T(1,128)}, u32[]{:S(2)}) copy-start(f32[1,1,256]{2,1,0:T(1,128)} %param.46) | copy-start | bytes 3076
  17.6 0.7 %copy-start.16 = (f32[19]{0:T(128)S(1)}, f32[19]{0:T(128)}, u32[]{:S(2)}) copy-start(f32[19]{0:T(128)} %ln_ref.1) | copy-start | bytes 232
  18.3 0.7 %copy-start.17 = (f32[19]{0:T(128)S(1)}, f32[19]{0:T(128)}, u32[]{:S(2)}) copy-start(f32[19]{0:T(128)} %kexp.1) | copy-start | bytes 232
  18.9 0.7 %copy-start.18 = (f32[19]{0:T(128)S(1)}, f32[19]{0:T(128)}, u32[]{:S(2)}) copy-start(f32[19]{0:T(128)} %energy.1) | copy-start | bytes 232

commit v2 on v1

--- a/solution.py
+++ b/solution.py
@@ -11,7 +11,7 @@
 F32 = jnp.float32
 B16 = jnp.bfloat16
 MESH = pl.DeviceIdType.MESH
-LANES = 128
+INS = 24
 
 
 def shift_of(n):
@@ -37,6 +37,12 @@
 
 def fdot(a, b):
     return jnp.dot(a, b, precision=HI, preferred_element_type=F32)
+
+
+def fdot_t(a, b):
+    return lax.dot_general(
+        a, b, (((1,), (1,)), ((), ())), precision=HI, preferred_element_type=F32
+    )
 
 
 def bdot(a, b):
@@ -60,53 +66,74 @@
     n_gx,
     n_gy,
     rows_x,
-    sp,
-    motion,
-    g_main,
-    g_cross,
-    vol,
-    kelvin,
-    dx,
-    cx,
-    bx,
-    mx,
-    dy,
-    cy,
-    by,
-    my,
-    ln_ref,
-    kexp,
-    energy,
-    flags,
-    stoich,
-    supply,
-    target,
-    used,
-    weight,
-    q,
-    ex_all,
-    ey_all,
-    wall_out,
-    wall_in,
-    fx_h,
-    fx_l,
-    fy_h,
-    fy_l,
-    u_h,
-    u_l,
-    acc,
-    x_send,
-    x_recv,
-    y_send,
-    y_recv,
-    w_send,
-    w_recv,
+    *refs,
 ):
+    held = refs[-INS:]
+    incoming_sem = refs[-INS - 1]
+    (
+        q,
+        fluid_out,
+        ex_all,
+        ey_all,
+        wall_out,
+        wall_in,
+        fx_h,
+        fx_l,
+        fy_h,
+        fy_l,
+        u_h,
+        u_l,
+        acc,
+        x_send,
+        x_recv,
+        y_send,
+        y_recv,
+        w_send,
+        w_recv,
+    ) = refs[INS : -INS - 1]
+    (
+        sp,
+        motion,
+        g_main,
+        g_cross,
+        vol,
+        kelvin,
+        dx,
+        cx,
+        bx,
+        mx,
+        dy,
+        cy,
+        by,
+        my,
+        ln_ref,
+        kexp,
+        energy,
+        flags,
+        stoich,
+        supply,
+        target,
+        used,
+        weight,
+        fluid,
+    ) = held
+    loads = {
+        id(dst): pltpu.make_async_copy(src, dst, incoming_sem.at[i])
+        for i, (src, dst) in enumerate(zip(refs[:INS], held))
+    }
+    first = (sp, motion, g_main, g_cross, cx, cy, supply, used, weight)
+    for ref in first + tuple(ref for ref in held if all(ref is not other for other in first)):
+        loads[id(ref)].start()
+
+    def arrive(*some):
+        for ref in some:
+            loads[id(ref)].wait()
+
     species, rows, lanes = sp.shape
     planes = rows // rows_x
     unknowns = cx.shape[0]
     slots = supply.shape[1]
-    reactions = flags.shape[0]
+    reactions = flags.shape[1]
     padded = ey_all.shape[1]
     me_x, me_y, me_z = lax.axis_index("gx"), lax.axis_index("gy"), lax.axis_index("gz")
 
@@ -128,6 +155,7 @@
     def part(s):
         return slice(s * lanes, (s + 1) * lanes)
 
+    arrive(sp, motion, g_main, g_cross, cx)
     contra_x = g_main[0] * motion[0] + g_cross[0] * motion[1]
     for s in range(species):
         fx_h[:, part(s)], fx_l[:, part(s)] = split(contra_x * sp[s])
@@ -159,6 +187,7 @@
     for s in range(species):
         fy_h[:, part(s)], fy_l[:, part(s)] = split(contra_y * sp[s])
     sel = ones_where(rest(iota((lanes, unknowns), 0), unknowns) == iota((lanes, unknowns), 1))
+    arrive(cy)
     cy_t = fdot(sel, cy[...]).T
     owner = over(iota((lanes, lanes), 1), unknowns)
     cy_h, cy_l = split(
@@ -182,6 +211,7 @@
     def down(row):
         return jnp.broadcast_to(row, (lanes, slots)).T
 
+    arrive(supply, used, weight)
     supply_col = down(supply[...])
     carried = down(weight[...] * used[...].astype(F32))
     wide = jnp.concatenate([over(supply_col, lanes)] * (rows // lanes), axis=1)
@@ -208,6 +238,7 @@
     w_copy.start()
 
     chunk = 16
+    arrive(kelvin, ln_ref, kexp, energy, flags, stoich)
 
     def chemistry(i, carry):
         at = pl.ds(pl.multiple_of(i * chunk, chunk), chunk)
@@ -219,16 +250,18 @@
         for r in range(reactions):
             value = ln_ref[r] + kexp[r] * ln_t - energy[r] * rec_t
             for s in range(species):
-                value = value + flags[r, s].astype(F32) * logs[s]
+                value = value + flags[s, r].astype(F32) * logs[s]
             progress = jnp.exp(value)
             for s in range(species):
-                sums[s] = sums[s] + stoich[r, s].astype(F32) * progress
+                sums[s] = sums[s] + stoich[s, r].astype(F32) * progress
         for s in range(species):
             q[s, at, :] = F32(0.2) * sums[s]
         return carry
 
     lax.fori_loop(0, rows // chunk, chemistry, 0)
 
+    arrive(dx, dy, target, vol, bx, mx, by, my, fluid)
+    fluid_out[...] = fluid[...].astype(F32)
     same = over(iota((rows, rows), 0), rows_x) == over(iota((rows, rows), 1), rows_x)
     dx_big = jnp.where(same, fdot(fdot(pick, dx[...]), pick_t), F32(0))
     acc[...] = dot3(split(dx_big), (fx_h[...], fx_l[...]))
@@ -255,16 +288,11 @@
     for s in range(species):
         q[s] += far_wall[:, part(s)]
 
-    wy = fdot(by[...], my[...])
     pieces = []
     for i in range(n_gy):
         shape = (padded, n_gy * unknowns)
         sel = ones_where(rest(iota(shape, 0), unknowns) + i * unknowns == iota(shape, 1))
-        pieces.append(
-            lax.dot_general(
-                sel, wy, (((1,), (1,)), ((), ())), precision=HI, preferred_element_type=F32
-            )
-        )
+        pieces.append(fdot(fdot_t(sel, my[...]), by[...]))
     base = jnp.concatenate(pieces, axis=0)
     owner = jnp.concatenate([over(iota((padded, lanes), 0), unknowns)] * n_gy, axis=0)
     wy_big = jnp.concatenate(
@@ -278,7 +306,7 @@
     count = n_gx * unknowns
     wide = count * planes
     sel = ones_where(over(iota((count, wide), 1), planes) == iota((count, wide), 0))
-    wx = fdot(pick, fdot(fdot(bx[...], mx[...]), sel))
+    wx = fdot(fdot_t(pick, bx[...]), fdot(mx[...], sel))
     wx_big = split(
         jnp.where(
             over(iota((rows, wide), 0), rows_x) == rest(iota((rows, wide), 1), planes), wx, F32(0)
@@ -297,27 +325,35 @@
 
 def per_device(n_gx, n_gy, *args):
     species_partial_mass = args[0]
-    open_volume_flags = args[-1]
     species, planes, rows_x, lanes = species_partial_mass.shape
     rows = planes * rows_x
     ins = [
         species_partial_mass.reshape(species, rows, lanes),
         *(a.reshape(2, rows, lanes) for a in args[1:4]),
         *(a.reshape(rows, lanes) for a in args[4:6]),
-        *args[6:19],
+        *args[6:8],
+        args[8].T,
+        *args[9:12],
+        args[12].T,
+        *args[13:17],
+        args[17].T,
+        args[18].T,
         *(a.reshape(1, -1) for a in args[19:23]),
+        args[23].reshape(rows, lanes),
     ]
-    slots = ins[-1].shape[1]
+    slots = ins[-2].shape[1]
     unknowns = args[7].shape[0]
     padded = -(-species * unknowns // 16) * 16
     wide = species * lanes
-    vmem = pl.BlockSpec(memory_space=pltpu.VMEM)
-    smem = pl.BlockSpec(memory_space=pltpu.SMEM)
-    q = pl.pallas_call(
+    spaces = [pltpu.VMEM] * 14 + [pltpu.SMEM] * 5 + [pltpu.VMEM] * 5
+    q, fluid = pl.pallas_call(
         functools.partial(kernel, n_gx, n_gy, rows_x),
-        out_shape=jax.ShapeDtypeStruct((species, rows, lanes), F32),
-        in_specs=[vmem] * 14 + [smem] * 5 + [vmem] * 4,
-        out_specs=vmem,
+        out_shape=(
+            jax.ShapeDtypeStruct((species, rows, lanes), F32),
+            jax.ShapeDtypeStruct((rows, lanes), F32),
+        ),
+        in_specs=[pl.BlockSpec(memory_space=pl.ANY)] * INS,
+        out_specs=[pl.BlockSpec(memory_space=pltpu.VMEM)] * 2,
         scratch_shapes=[
             pltpu.VMEM((n_gx, unknowns * planes, wide), F32),
             pltpu.VMEM((n_gy, padded, rows), F32),
@@ -332,13 +368,15 @@
             pltpu.SemaphoreType.DMA((n_gy,)),
             pltpu.SemaphoreType.DMA,
             pltpu.SemaphoreType.DMA,
+            pltpu.SemaphoreType.DMA((INS,)),
+            *(space(a.shape, a.dtype) for space, a in zip(spaces, ins)),
         ],
         compiler_params=pltpu.CompilerParams(
-            collective_id=0, has_side_effects=True, vmem_limit_bytes=48 * 2**20
+            collective_id=0, has_side_effects=True, vmem_limit_bytes=56 * 2**20
         ),
     )(*ins)
     q = q.reshape(species_partial_mass.shape)
-    section_rhs = open_volume_flags.astype(F32)[None] * q
+    section_rhs = fluid.reshape(planes, rows_x, lanes)[None] * q
     section_state = species_partial_mass + 0.25 * section_rhs
     return (section_rhs, section_state)
 

time: 41.5 us -> 25.2 us (0.61); the launches traced: 40.8 us -> 25.1 us
  local copies, waits for them, and re-layouts: 18 us -> 0.01 us
  Pallas kernels: 19.4 us -> 21.4 us
    unnamed x42 -> x2, local copies, waits for them, and re-layouts: 18 us -> 0.01 us
    pallas_call x1, Pallas kernels: 19.4 us -> 21.4 us  [per_device(): pl.pallas_call(functools.partial(kernel, n_gx, n_gy, rows_x), out_shape=(...]
    add x1, other arithmetic: 1.73 us -> 3.05 us  [per_device(): section_state = species_partial_mass + 0.25 * section_rhs]
    convert_element_type x1 -> x0, other arithmetic: 0.91 us -> none  [per_device(): section_rhs = open_volume_flags.astype(F32)[None] * q]
where the time goes in v2:
time: 25.2 us; the launch traced here: 25.1 us
  Pallas kernels  21.4 us (85%)
  other arithmetic  3.05 us (12%)
  between operations  0.66 us (3%)
    pallas_call x1, Pallas kernels, per_device(): pl.pallas_call(functools.partial(kernel, n_gx, n_gy, rows_x), out_shape=(...  21.4 us
    add x1, other arithmetic, per_device(): section_state = species_partial_mass + 0.25 * section_rhs  3.05 us

profile of v2, /device:TPU:0, one launch (start us, length us, event | category | flops | bytes accessed | tf_op | source)
XLA Modules:
  0.0 25.1 jit_solution(6823373902584928824)
XLA Ops:
  0.6 0.0 copy-start
  0.7 21.4 %shard_map.239 = (f32[9,256,128]{2,1,0:T(8,128)}, f32[256,128]{1,0:T(8,128)}) custom-call(f32[9,256,128]{2,1,0:T(8,128)} %bitcast.17, f32[2,256,128]{2,1,0:T(8,128)} %bitcast.19, f32[2,256,128]{2,1,0:T(8,128)} %bitcast.20, f32[2,256,128]{2,1,0:T(8,128)} %bitcast.21, f32[256,128]{1,0:T(8,128)} %bitcast.22, f32[256,128]{1,0:T(8,128)} %bitcast.23, ...), custom_call_target="tpu_custom_call" | custom-call | tf_op jit(solution)/shard_map/pallas_call | solution.py:349
  22.0 0.0 copy-done
  22.0 3.0 %multiply_add_fusion = (f32[9,8,32,128]{3,2,1,0:T(8,128)}, f32[9,8,32,128]{3,2,1,0:T(8,128)}) fusion(f32[9,8,32,128]{3,2,1,0:T(8,128)S(1)} %copy-done, f32[9,8,32,128]{3,2,1,0:T(8,128)} %bitcast.18, f32[8,32,128]{2,1,0:T(8,128)} %bitcast.25), kind=kLoop, calls=%fused_computation | loop fusion | flops 884736 | bytes 4849664 | tf_op jit(solution)/shard_map/add | solution.py:380
Async XLA Ops:
  0.6 21.4 %copy-start = (f32[9,8,32,128]{3,2,1,0:T(8,128)S(1)}, f32[9,8,32,128]{3,2,1,0:T(8,128)}, u32[]{:S(2)}) copy-start(f32[9,8,32,128]{3,2,1,0:T(8,128)} %param.24) | copy-start | bytes 3538948

commit v3 on v2

--- a/solution.py
+++ b/solution.py
@@ -12,6 +12,7 @@
 B16 = jnp.bfloat16
 MESH = pl.DeviceIdType.MESH
 INS = 24
+GROUP = 8
 
 
 def shift_of(n):
@@ -193,7 +194,8 @@
     cy_h, cy_l = split(
         jnp.concatenate([jnp.where(owner == s, cy_t, F32(0)) for s in range(species)], axis=0)
     )
-    ey = dot3((fy_h[...], fy_l[...]), (cy_h, cy_l))
+    both = bdot(fy_h[...], jnp.concatenate([cy_h, cy_l], axis=1))
+    ey = both[:, :lanes] + both[:, lanes:] + bdot(fy_l[...], cy_h)
     ey_all[me_y] = ey.T[:padded]
     y_copies = []
     for d in range(1, n_gy):
@@ -237,25 +239,67 @@
     )
     w_copy.start()
 
-    chunk = 16
     arrive(kelvin, ln_ref, kexp, energy, flags, stoich)
+    high, deep = reactions * GROUP, species * GROUP
+    sel_r = ones_where(over(iota((high, reactions), 0), GROUP) == iota((high, reactions), 1))
+    sel_s = ones_where(over(iota((species, deep), 1), GROUP) == iota((species, deep), 0))
+    consumed = jnp.where(
+        rest(iota((high, deep), 0), GROUP) == rest(iota((high, deep), 1), GROUP),
+        fdot(fdot_t(sel_r, flags[...].astype(F32)), sel_s),
+        F32(0),
+    )
+    sel_s = ones_where(over(iota((deep, species), 0), GROUP) == iota((deep, species), 1))
+    sel_r_t = ones_where(over(iota((reactions, high), 1), GROUP) == iota((reactions, high), 0))
+    shifts = jnp.where(
+        rest(iota((deep, high), 0), GROUP) == rest(iota((deep, high), 1), GROUP),
+        fdot(fdot(sel_s, stoich[...].astype(F32)), sel_r_t),
+        F32(0),
+    ).astype(B16)
+
+    def pieces_of(value):
+        top = value.astype(B16).astype(F32)
+        return top, value - top
+
+    def each_reaction(row):
+        column = jnp.sum(sel_r * row, axis=1, keepdims=True)
+        return pieces_of(
+            jnp.where(
+                rest(iota((high, GROUP), 0), GROUP) == iota((high, GROUP), 1), column, F32(0)
+            )
+        )
+
+    k_h, k_l = each_reaction(kexp[...])
+    e_h, e_l = each_reaction(-energy[...])
+    a_h, a_l = each_reaction(ln_ref[...])
+    exponents = jnp.concatenate(
+        [consumed, consumed, k_h, k_h, k_l, e_h, e_h, e_l, a_h, a_l], axis=1
+    ).astype(B16)
+    groups = 8
+    chunk = groups * GROUP
+
+    def side_by_side(value):
+        return jnp.concatenate(
+            [value[g * GROUP : (g + 1) * GROUP] for g in range(groups)], axis=1
+        )
 
     def chemistry(i, carry):
         at = pl.ds(pl.multiple_of(i * chunk, chunk), chunk)
-        temperature = kelvin[at, :]
-        ln_t = jnp.log(temperature / F32(1500.0))
-        rec_t = F32(1.0) / temperature - F32(1.0 / 1500.0)
-        logs = [jnp.log(sp[s, at, :]) for s in range(species)]
-        sums = [jnp.zeros((chunk, lanes), F32) for _ in range(species)]
-        for r in range(reactions):
-            value = ln_ref[r] + kexp[r] * ln_t - energy[r] * rec_t
-            for s in range(species):
-                value = value + flags[s, r].astype(F32) * logs[s]
-            progress = jnp.exp(value)
-            for s in range(species):
-                sums[s] = sums[s] + stoich[s, r].astype(F32) * progress
+        temperature = side_by_side(kelvin[at, :])
+        t_h, t_l = pieces_of(jnp.log(temperature / F32(1500.0)))
+        r_h, r_l = pieces_of(F32(1.0) / temperature - F32(1.0 / 1500.0))
+        logs = [pieces_of(jnp.log(side_by_side(sp[s, at, :]))) for s in range(species)]
+        one = jnp.ones_like(temperature)
+        stacked = jnp.concatenate(
+            [x[0] for x in logs]
+            + [x[1] for x in logs]
+            + [t_h, t_l, t_h, r_h, r_l, r_h, one, one],
+            axis=0,
+        ).astype(B16)
+        progress = jnp.exp(bdot(exponents, stacked))
+        made = F32(0.2) * dot2(shifts, split(progress))
         for s in range(species):
-            q[s, at, :] = F32(0.2) * sums[s]
+            row = made[s * GROUP : (s + 1) * GROUP]
+            q[s, at, :] = jnp.concatenate([row[:, part(g)] for g in range(groups)], axis=0)
         return carry
 
     lax.fori_loop(0, rows // chunk, chemistry, 0)
@@ -265,9 +309,17 @@
     same = over(iota((rows, rows), 0), rows_x) == over(iota((rows, rows), 1), rows_x)
     dx_big = jnp.where(same, fdot(fdot(pick, dx[...]), pick_t), F32(0))
     acc[...] = dot3(split(dx_big), (fx_h[...], fx_l[...]))
-    dy_t = split(dy[...].T)
-    for s in range(species):
-        acc[:, part(s)] += dot3((fy_h[:, part(s)], fy_l[:, part(s)]), dy_t)
+    dy_h, dy_l = split(dy[...].T)
+    dy_two = jnp.concatenate(
+        [
+            jnp.concatenate([dy_h, dy_h], axis=0),
+            jnp.concatenate([dy_l, jnp.zeros_like(dy_l)], axis=0),
+        ],
+        axis=1,
+    )
+    for s in range(species):
+        both = bdot(jnp.concatenate([fy_h[:, part(s)], fy_l[:, part(s)]], axis=1), dy_two)
+        acc[:, part(s)] += both[:, :lanes] + both[:, lanes:]
 
     to_supply = ones_where(
         over(jnp.broadcast_to(supply[...], (rows, slots)), lanes) == iota((rows, slots), 0)
@@ -307,15 +359,18 @@
     wide = count * planes
     sel = ones_where(over(iota((count, wide), 1), planes) == iota((count, wide), 0))
     wx = fdot(fdot_t(pick, bx[...]), fdot(mx[...], sel))
-    wx_big = split(
+    wx_h, wx_l = split(
         jnp.where(
             over(iota((rows, wide), 0), rows_x) == rest(iota((rows, wide), 1), planes), wx, F32(0)
         )
     )
     for copy in x_copies:
         copy.wait_recv()
-    ex = split(ex_all[...].reshape(wide, species * lanes))
-    total = acc[...] + dot3(wx_big, ex)
+    ex_h, ex_l = split(ex_all[...].reshape(wide, species * lanes))
+    total = acc[...] + bdot(wx_l, ex_h)
+    total += bdot(
+        jnp.concatenate([wx_h, wx_h], axis=1), jnp.concatenate([ex_h, ex_l], axis=0)
+    )
     for s in range(species):
         q[s] = q[s] - vol[...] * total[:, part(s)]
 
@@ -335,7 +390,8 @@
         args[8].T,
         *args[9:12],
         args[12].T,
-        *args[13:17],
+        args[13],
+        *(a.reshape(1, -1) for a in args[14:17]),
         args[17].T,
         args[18].T,
         *(a.reshape(1, -1) for a in args[19:23]),
@@ -345,7 +401,6 @@
     unknowns = args[7].shape[0]
     padded = -(-species * unknowns // 16) * 16
     wide = species * lanes
-    spaces = [pltpu.VMEM] * 14 + [pltpu.SMEM] * 5 + [pltpu.VMEM] * 5
     q, fluid = pl.pallas_call(
         functools.partial(kernel, n_gx, n_gy, rows_x),
         out_shape=(
@@ -369,7 +424,7 @@
             pltpu.SemaphoreType.DMA,
             pltpu.SemaphoreType.DMA,
             pltpu.SemaphoreType.DMA((INS,)),
-            *(space(a.shape, a.dtype) for space, a in zip(spaces, ins)),
+            *(pltpu.VMEM(a.shape, a.dtype) for a in ins),
         ],
         compiler_params=pltpu.CompilerParams(
             collective_id=0, has_side_effects=True, vmem_limit_bytes=56 * 2**20

time: 25.2 us -> 23.6 us (0.937)
  Pallas kernels: 21.4 us -> 19.7 us
    pallas_call x1, Pallas kernels: 21.4 us -> 19.7 us  [per_device(): pl.pallas_call(functools.partial(kernel, n_gx, n_gy, rows_x), out_shape=(...]
where the time goes in v3:
time: 23.6 us; the launch traced here: 23.4 us
  Pallas kernels  19.7 us (83%)
  other arithmetic  3.05 us (13%)
  between operations  0.66 us (3%)
    pallas_call x1, Pallas kernels, per_device(): pl.pallas_call(functools.partial(kernel, n_gx, n_gy, rows_x), out_shape=(...  19.7 us
    add x1, other arithmetic, per_device(): section_state = species_partial_mass + 0.25 * section_rhs  3.05 us

profile of v3, /device:TPU:0, one launch (start us, length us, event | category | flops | bytes accessed | tf_op | source)
XLA Modules:
  0.0 23.4 jit_solution(15478785082666573705)
XLA Ops:
  0.6 0.0 copy-start
  0.7 19.7 %shard_map.239 = (f32[9,256,128]{2,1,0:T(8,128)}, f32[256,128]{1,0:T(8,128)}) custom-call(f32[9,256,128]{2,1,0:T(8,128)} %bitcast.20, f32[2,256,128]{2,1,0:T(8,128)} %bitcast.22, f32[2,256,128]{2,1,0:T(8,128)} %bitcast.23, f32[2,256,128]{2,1,0:T(8,128)} %bitcast.24, f32[256,128]{1,0:T(8,128)} %bitcast.25, f32[256,128]{1,0:T(8,128)} %bitcast.26, ...), custom_call_target="tpu_custom_call" | custom-call | tf_op jit(solution)/shard_map/pallas_call | solution.py:404
  20.4 0.0 copy-done
  20.4 3.0 %multiply_add_fusion = (f32[9,8,32,128]{3,2,1,0:T(8,128)}, f32[9,8,32,128]{3,2,1,0:T(8,128)}) fusion(f32[9,8,32,128]{3,2,1,0:T(8,128)S(1)} %copy-done, f32[9,8,32,128]{3,2,1,0:T(8,128)} %bitcast.21, f32[8,32,128]{2,1,0:T(8,128)} %bitcast.28), kind=kLoop, calls=%fused_computation | loop fusion | flops 884736 | bytes 4849664 | tf_op jit(solution)/shard_map/add | solution.py:435
Async XLA Ops:
  0.6 19.7 %copy-start = (f32[9,8,32,128]{3,2,1,0:T(8,128)S(1)}, f32[9,8,32,128]{3,2,1,0:T(8,128)}, u32[]{:S(2)}) copy-start(f32[9,8,32,128]{3,2,1,0:T(8,128)} %param.24) | copy-start | bytes 3538948

commit v4 on v3

--- a/solution.py
+++ b/solution.py
@@ -122,7 +122,7 @@
         id(dst): pltpu.make_async_copy(src, dst, incoming_sem.at[i])
         for i, (src, dst) in enumerate(zip(refs[:INS], held))
     }
-    first = (sp, motion, g_main, g_cross, cx, cy, supply, used, weight)
+    first = (cx, cy, sp, motion, g_main, g_cross, supply, used, weight)
     for ref in first + tuple(ref for ref in held if all(ref is not other for other in first)):
         loads[id(ref)].start()
 
@@ -156,10 +156,7 @@
     def part(s):
         return slice(s * lanes, (s + 1) * lanes)
 
-    arrive(sp, motion, g_main, g_cross, cx)
-    contra_x = g_main[0] * motion[0] + g_cross[0] * motion[1]
-    for s in range(species):
-        fx_h[:, part(s)], fx_l[:, part(s)] = split(contra_x * sp[s])
+    arrive(cx, cy)
     pick = ones_where(rest(iota((rows, rows_x), 0), rows_x) == iota((rows, rows_x), 1))
     pick_t = ones_where(rest(iota((rows_x, rows), 1), rows_x) == iota((rows_x, rows), 0))
     side = unknowns * planes
@@ -169,7 +166,21 @@
         fdot(fdot(sel, cx[...]), pick_t),
         F32(0),
     )
-    ex_all[me_x] = dot3(split(cx_big), (fx_h[...], fx_l[...]))
+    cx_h, cx_l = split(cx_big)
+    cx_two = jnp.concatenate([cx_h, cx_l], axis=0)
+    sel = ones_where(rest(iota((lanes, unknowns), 0), unknowns) == iota((lanes, unknowns), 1))
+    cy_t = fdot(sel, cy[...]).T
+    owner = over(iota((lanes, lanes), 1), unknowns)
+    cy_h, cy_l = split(
+        jnp.concatenate([jnp.where(owner == s, cy_t, F32(0)) for s in range(species)], axis=0)
+    )
+
+    arrive(sp, motion, g_main, g_cross)
+    contra_x = g_main[0] * motion[0] + g_cross[0] * motion[1]
+    for s in range(species):
+        fx_h[:, part(s)], fx_l[:, part(s)] = split(contra_x * sp[s])
+    both = bdot(cx_two, fx_h[...])
+    ex_all[me_x] = both[:side] + both[side:] + bdot(cx_h, fx_l[...])
     pl.semaphore_wait(barrier, n_gx + n_gy - 1)
     x_copies = []
     for d in range(1, n_gx):
@@ -187,13 +198,6 @@
     contra_y = g_cross[1] * motion[0] + g_main[1] * motion[1]
     for s in range(species):
         fy_h[:, part(s)], fy_l[:, part(s)] = split(contra_y * sp[s])
-    sel = ones_where(rest(iota((lanes, unknowns), 0), unknowns) == iota((lanes, unknowns), 1))
-    arrive(cy)
-    cy_t = fdot(sel, cy[...]).T
-    owner = over(iota((lanes, lanes), 1), unknowns)
-    cy_h, cy_l = split(
-        jnp.concatenate([jnp.where(owner == s, cy_t, F32(0)) for s in range(species)], axis=0)
-    )
     both = bdot(fy_h[...], jnp.concatenate([cy_h, cy_l], axis=1))
     ey = both[:, :lanes] + both[:, lanes:] + bdot(fy_l[...], cy_h)
     ey_all[me_y] = ey.T[:padded]

time: 23.6 us -> 23.6 us (level)
  no operation moved by 1% of the time
where the time goes in v4:
time: 23.6 us; the launch traced here: 23.4 us
  Pallas kernels  19.7 us (83%)
  other arithmetic  3.05 us (13%)
  between operations  0.66 us (3%)
    pallas_call x1, Pallas kernels, per_device(): pl.pallas_call(functools.partial(kernel, n_gx, n_gy, rows_x), out_shape=(...  19.7 us
    add x1, other arithmetic, per_device(): section_state = species_partial_mass + 0.25 * section_rhs  3.05 us

profile of v4, /device:TPU:0, one launch (start us, length us, event | category | flops | bytes accessed | tf_op | source)
XLA Modules:
  0.0 23.4 jit_solution(6184970970922624148)
XLA Ops:
  0.6 0.0 copy-start
  0.7 19.7 %shard_map.239 = (f32[9,256,128]{2,1,0:T(8,128)}, f32[256,128]{1,0:T(8,128)}) custom-call(f32[9,256,128]{2,1,0:T(8,128)} %bitcast.20, f32[2,256,128]{2,1,0:T(8,128)} %bitcast.22, f32[2,256,128]{2,1,0:T(8,128)} %bitcast.23, f32[2,256,128]{2,1,0:T(8,128)} %bitcast.24, f32[256,128]{1,0:T(8,128)} %bitcast.25, f32[256,128]{1,0:T(8,128)} %bitcast.26, ...), custom_call_target="tpu_custom_call" | custom-call | tf_op jit(solution)/shard_map/pallas_call | solution.py:408
  20.4 0.0 copy-done
  20.4 3.0 %multiply_add_fusion = (f32[9,8,32,128]{3,2,1,0:T(8,128)}, f32[9,8,32,128]{3,2,1,0:T(8,128)}) fusion(f32[9,8,32,128]{3,2,1,0:T(8,128)S(1)} %copy-done, f32[9,8,32,128]{3,2,1,0:T(8,128)} %bitcast.21, f32[8,32,128]{2,1,0:T(8,128)} %bitcast.28), kind=kLoop, calls=%fused_computation | loop fusion | flops 884736 | bytes 4849664 | tf_op jit(solution)/shard_map/add | solution.py:439
Async XLA Ops:
  0.6 19.7 %copy-start = (f32[9,8,32,128]{3,2,1,0:T(8,128)S(1)}, f32[9,8,32,128]{3,2,1,0:T(8,128)}, u32[]{:S(2)}) copy-start(f32[9,8,32,128]{3,2,1,0:T(8,128)} %param.24) | copy-start | bytes 3538948

commit v5 on v4

--- a/solution.py
+++ b/solution.py
@@ -278,7 +278,7 @@
     exponents = jnp.concatenate(
         [consumed, consumed, k_h, k_h, k_l, e_h, e_h, e_l, a_h, a_l], axis=1
     ).astype(B16)
-    groups = 8
+    groups = 16
     chunk = groups * GROUP
 
     def side_by_side(value):

time: 23.6 us -> 23.6 us (level)
  no operation moved by 1% of the time
where the time goes in v5:
time: 23.6 us; the launch traced here: 23.4 us
  Pallas kernels  19.7 us (83%)
  other arithmetic  3.05 us (13%)
  between operations  0.66 us (3%)
    pallas_call x1, Pallas kernels, per_device(): pl.pallas_call(functools.partial(kernel, n_gx, n_gy, rows_x), out_shape=(...  19.7 us
    add x1, other arithmetic, per_device(): section_state = species_partial_mass + 0.25 * section_rhs  3.05 us

profile of v5, /device:TPU:0, one launch (start us, length us, event | category | flops | bytes accessed | tf_op | source)
XLA Modules:
  0.0 23.4 jit_solution(3155651840601565189)
XLA Ops:
  0.6 0.0 copy-start
  0.7 19.7 %shard_map.239 = (f32[9,256,128]{2,1,0:T(8,128)}, f32[256,128]{1,0:T(8,128)}) custom-call(f32[9,256,128]{2,1,0:T(8,128)} %bitcast.20, f32[2,256,128]{2,1,0:T(8,128)} %bitcast.22, f32[2,256,128]{2,1,0:T(8,128)} %bitcast.23, f32[2,256,128]{2,1,0:T(8,128)} %bitcast.24, f32[256,128]{1,0:T(8,128)} %bitcast.25, f32[256,128]{1,0:T(8,128)} %bitcast.26, ...), custom_call_target="tpu_custom_call" | custom-call | tf_op jit(solution)/shard_map/pallas_call | solution.py:408
  20.4 0.0 copy-done
  20.4 3.0 %multiply_add_fusion = (f32[9,8,32,128]{3,2,1,0:T(8,128)}, f32[9,8,32,128]{3,2,1,0:T(8,128)}) fusion(f32[9,8,32,128]{3,2,1,0:T(8,128)S(1)} %copy-done, f32[9,8,32,128]{3,2,1,0:T(8,128)} %bitcast.21, f32[8,32,128]{2,1,0:T(8,128)} %bitcast.28), kind=kLoop, calls=%fused_computation | loop fusion | flops 884736 | bytes 4849664 | tf_op jit(solution)/shard_map/add | solution.py:439
Async XLA Ops:
  0.6 19.7 %copy-start = (f32[9,8,32,128]{3,2,1,0:T(8,128)S(1)}, f32[9,8,32,128]{3,2,1,0:T(8,128)}, u32[]{:S(2)}) copy-start(f32[9,8,32,128]{3,2,1,0:T(8,128)} %param.24) | copy-start | bytes 3538948
